TPU v7x, 32 devices: a whole 2x2x4 slice. The times are simulated.
32 devices in a mesh: expert: 8 (over z, y), dp: 4 (over x, core).
Axes of the slice: x: 2, y: 2, z: 4, core: 2. Of those that a mesh axis runs over, the one named last changes fastest.
Arguments:
- inputs: bfloat16 [4096, 1024], P(('expert', 'dp')), may hold values from -6 to 6
- out_grad: bfloat16 [4096, 1024], P(('expert', 'dp')), may hold values from -6 to 6
- expert_ids: int32 [4096, 2], P(('expert', 'dp')), may hold values from 0 to 7, as said below
- slot_ids: int32 [4096, 2], P(('expert', 'dp')), may hold values from -1 to 31, as said below
- gate_values: bfloat16 [4096, 2], P(('expert', 'dp')), may hold values from 0.099609375 to 0.8984375
- first_layer: bfloat16 [8, 1024, 4096], P('expert', None, 'dp'), may hold values from -0.1875 to 0.1875
- second_layer: bfloat16 [8, 4096, 1024], P('expert', 'dp'), may hold values from -0.09375 to 0.09375
Outputs:
- input_grad: bfloat16 [4096, 1024], P(('expert', 'dp'))
- gate_grad: bfloat16 [4096, 2], P(('expert', 'dp'))
- first_grad: bfloat16 [8, 1024, 4096], P('expert', None, 'dp')
- second_grad: bfloat16 [8, 4096, 1024], P('expert', 'dp')
Inputs may be any that keep to these rules, and one draw needn't show every extreme that they name: `expert_ids`: the two experts of a token differ. slot_ids[t, k] is the number of assignments to expert expert_ids[t, k] from the token's group that come before it, where all first assignments of the group come before all second ones, in token order; it is -1 where that number is 32 or more. No two kept assignments of a group share an expert and a slot.
All inputs are finite; a program needn't handle non-finite values.
Results may differ from a plain program's by a relative error of at most 0.008.
Values may be sent and summed in bfloat16 or wider, within the bound.
A program may use at most 128 MiB of HBM per device.

v0:
```python
import math

import jax
import jax.numpy as jnp
from jax import lax
from jax.sharding import PartitionSpec as P

coef_root = math.sqrt(2.0 / math.pi)


def gelu_pair(pre_value):
    cubic_term = 0.044715 * pre_value * pre_value * pre_value
    tanh_part = jnp.tanh(coef_root * (pre_value + cubic_term))
    activation = 0.5 * pre_value * (1.0 + tanh_part)
    derivative = 0.5 * (1.0 + tanh_part) + 0.5 * pre_value * (
        1.0 - tanh_part * tanh_part
    ) * coef_root * (1.0 + 3.0 * 0.044715 * pre_value * pre_value)
    return (activation, derivative)


def slot_tables(expert_ids, slot_ids, gate_values, experts, capacity):
    tok_count = expert_ids.shape[0]
    position = jnp.where(slot_ids >= 0, expert_ids * capacity + slot_ids, experts * capacity)
    flat_slots = position.reshape(-1)
    owners = jnp.repeat(jnp.arange(tok_count, dtype=jnp.int32), expert_ids.shape[1])
    owner_table = (
        jnp.full((experts * capacity,), tok_count, jnp.int32)
        .at[flat_slots]
        .set(owners, mode="drop")
    )
    gate_table = (
        jnp.zeros((experts * capacity,), gate_values.dtype)
        .at[flat_slots]
        .set(gate_values.reshape(-1), mode="drop")
    )
    return (position, owner_table, gate_table)


def build_slots(inputs, out_grad, expert_ids, slot_ids, gate_values, experts, capacity):
    position, owner_table, gate_table = slot_tables(
        expert_ids, slot_ids, gate_values, experts, capacity
    )
    feat_width = inputs.shape[1]
    dispatched = jnp.take(inputs, owner_table, axis=0, mode="fill", fill_value=0).reshape(
        experts, capacity, feat_width
    )
    cotangent = jnp.take(out_grad, owner_table, axis=0, mode="fill", fill_value=0).reshape(
        experts, capacity, feat_width
    )
    return (position, dispatched, cotangent, gate_table.reshape(experts, capacity))


def expert_work(slot_in, slot_cot, slot_gate, layer_in, layer_out):
    pre = jnp.dot(slot_in, layer_in, preferred_element_type=jnp.float32)
    act_full, derivative = gelu_pair(pre)
    activation = act_full.astype(jnp.bfloat16)
    back = lax.dot_general(
        slot_cot, layer_out, (((1,), (1,)), ((), ())), preferred_element_type=jnp.float32
    )
    inner_dot = jnp.sum(activation.astype(jnp.float32) * back, axis=1)
    gate_col = slot_gate.astype(jnp.float32)[:, None]
    scaled = (gate_col * slot_cot.astype(jnp.float32)).astype(jnp.bfloat16)
    hidden_grad = (gate_col * back * derivative).astype(jnp.bfloat16)
    in_grad = lax.dot_general(
        slot_in, hidden_grad, (((0,), (0,)), ((), ())), preferred_element_type=jnp.float32
    ).astype(jnp.bfloat16)
    out_grad_w = lax.dot_general(
        activation, scaled, (((0,), (0,)), ((), ())), preferred_element_type=jnp.float32
    ).astype(jnp.bfloat16)
    partial_value = lax.dot_general(
        hidden_grad, layer_in, (((1,), (1,)), ((), ())), preferred_element_type=jnp.float32
    )
    return (partial_value, inner_dot, in_grad, out_grad_w)


def per_device(inputs, out_grad, expert_ids, slot_ids, gate_values, first_layer, second_layer):
    experts = lax.axis_size("expert")
    tok_count = inputs.shape[0]
    feat_width = inputs.shape[1]
    capacity = expert_ids.shape[1] * tok_count // experts
    layer_in = first_layer[0]
    layer_out = second_layer[0]
    position, dispatched, cotangent, gate_slots = build_slots(
        inputs, out_grad, expert_ids, slot_ids, gate_values, experts, capacity
    )
    dispatched, cotangent, gate_slots = (
        lax.all_to_all(dispatched, "expert", split_axis=0, concat_axis=0, tiled=True),
        lax.all_to_all(cotangent, "expert", split_axis=0, concat_axis=0, tiled=True),
        lax.all_to_all(gate_slots, "expert", split_axis=0, concat_axis=0, tiled=True),
    )
    dispatched, cotangent, gate_slots = (
        lax.all_gather(dispatched.reshape(-1, feat_width), "dp", axis=0, tiled=True),
        lax.all_gather(cotangent.reshape(-1, feat_width), "dp", axis=0, tiled=True),
        lax.all_gather(gate_slots.reshape(-1), "dp", axis=0, tiled=True),
    )
    partial_value, inner_dot, first_grad, second_grad = expert_work(
        dispatched, cotangent, gate_slots, layer_in, layer_out
    )
    summed, inner_sum = (
        lax.psum_scatter(partial_value, "dp", scatter_dimension=0, tiled=True),
        lax.psum_scatter(inner_dot, "dp", scatter_dimension=0, tiled=True),
    )
    slot_grad = summed.astype(jnp.bfloat16).reshape(experts, capacity, feat_width)
    slot_inner = inner_sum.astype(jnp.bfloat16).reshape(experts, capacity)
    slot_grad, slot_inner = (
        lax.all_to_all(slot_grad, "expert", split_axis=0, concat_axis=0, tiled=True),
        lax.all_to_all(slot_inner, "expert", split_axis=0, concat_axis=0, tiled=True),
    )
    slot_grad = slot_grad.reshape(experts * capacity, feat_width)
    slot_inner = slot_inner.reshape(experts * capacity)
    picked = jnp.take(slot_grad, position, axis=0, mode="fill", fill_value=0)
    input_grad = jnp.sum(picked.astype(jnp.float32), axis=1).astype(jnp.bfloat16)
    gate_grad = jnp.take(slot_inner, position, axis=0, mode="fill", fill_value=0)
    return (input_grad, gate_grad, first_grad[None], second_grad[None])


def solution(mesh):
    placed = (
        P(("expert", "dp"), None),
        P(("expert", "dp"), None),
        P(("expert", "dp"), None),
        P(("expert", "dp"), None),
        P(("expert", "dp"), None),
        P("expert", None, "dp"),
        P("expert", "dp", None),
    )
    return jax.shard_map(
        per_device,
        mesh=mesh,
        in_specs=placed,
        out_specs=(
            P(("expert", "dp"), None),
            P(("expert", "dp"), None),
            P("expert", None, "dp"),
            P("expert", "dp", None),
        ),
        check_vma=False,
    )
```

profile of v0, /device:TPU:0, one launch (start us, length us, event | category | flops | bytes accessed | tf_op | source)
XLA Modules:
  0.0 173.1 jit_solution(1119939727639421344)
XLA Ops:
  7.2 0.9 compare_select_fusion.2
  8.5 1.4 scatter_custom_fusion.1
  10.0 2.5 %gather_fusion.3 = bf16[256,1024]{1,0:T(8,128)(2,1)S(1)} fusion(bf16[128,1024]{1,0:T(8,128)(2,1)} %param.9, s32[1024]{0:T(1024)S(1)} %pad_clamp_fusion.1), kind=kCustom, calls=%fused_computation.1.clone | custom fusion | bytes 1049600 | tf_op jit(solution)/shard_map/jit(_take)/gather | solution.py:44
  12.5 1.2 gather_fusion.2
  13.7 0.9 broadcast_select_fusion.2
  14.7 21.7 %all_to_all.35 = bf16[8,32,1024]{2,1,0:T(8,128)(2,1)} all-to-all(bf16[8,32,1024]{2,1,0:T(8,128)(2,1)S(1)} %bitcast.32), channel_id=1, replica_groups=mesh['expert'=8,'dp'=4] {'expert'}, dimensions={0} | all-to-all | bytes 1048576 | tf_op jit(solution)/shard_map/all_to_all | solution.py:87
  36.4 17.7 %all_to_all.36 = bf16[8,32,1024]{2,1,0:T(8,128)(2,1)S(1)} all-to-all(bf16[8,32,1024]{2,1,0:T(8,128)(2,1)} %bitcast.31), channel_id=1, replica_groups=mesh['expert'=8,'dp'=4] {'expert'}, dimensions={0} | all-to-all | bytes 1048576 | tf_op jit(solution)/shard_map/all_to_all | solution.py:88
  54.2 1.0 copy.35
  55.5 2.2 %scatter_custom_fusion = bf16[256]{0:T(256)(128)(2,1)S(1)} fusion(s32[256]{0:T(256)S(1)} %bitcast.38, bf16[256]{0:T(256)(128)(2,1)S(1)} %reshape.137, bf16[]{:T(256)} %constant.27.clone.1), kind=kCustom, calls=%fused_computation.44 | custom fusion | bytes 514 | tf_op jit(solution)/shard_map/scatter | solution.py:34
  57.8 9.9 %all_to_all.37 = bf16[8,1,32]{2,1,0:T(2,128)(2,1)S(1)} all-to-all(bf16[8,1,32]{2,1,0:T(2,128)(2,1)S(1)} %all_to_all.28), channel_id=1, replica_groups=mesh['expert'=8,'dp'=4] {'expert'}, dimensions={0} | all-to-all | bytes 1024 | tf_op jit(solution)/shard_map/all_to_all | solution.py:89
  67.8 5.2 %all-gather = bf16[4,1,256]{2,1,0:T(2,128)(2,1)S(1)} all-gather(bf16[1,1,256]{2,1,0:T(2,128)(2,1)S(1)} %reshape.155), channel_id=1, replica_groups=mesh['expert'=8,'dp'=4] {'dp'}, dimensions={0}, use_global_device_ids=true | all-gather | bytes 2560 | tf_op jit(solution)/shard_map/all_gather | solution.py:94
  73.1 5.9 %fusion.10 = f32[1024,1024]{0,1:T(8,128)} fusion(bf16[1024,1024]{1,0:T(8,128)(2,1)} %all-gather.6.cloned.1.call-done, bf16[1,1024,1024]{2,1,0:T(8,128)(2,1)S(1)} %copy-done), kind=kOutput, calls=%fused_computation.21 | convolution fusion | flops 2147483648 | bytes 8388608 | tf_op jit(solution)/shard_map/dot_general | solution.py:54
  79.0 4.2 %all-gather.4.cloned.1.call-done = bf16[1024,1024]{0,1:T(8,128)(2,1)} async-done(((bf16[256,1024]{0,1:T(8,128)(2,1)}), bf16[1024,1024]{0,1:T(8,128)(2,1)}) %all-gather.4.cloned.1.call-update) | async-done | bytes 2097168 | tf_op jit(solution)/shard_map/all_gather | solution.py:93
  83.2 7.7 %multiply_reduce_fusion = (f32[1024]{0:T(1024)S(1)}, bf16[1024,1024]{0,1:T(8,128)(2,1)S(1)}) fusion(f32[1024,1024]{0,1:T(8,128)} %fusion.10, f32[1024]{0:T(1024)S(1)} %bitcast.35, bf16[1024,1024]{0,1:T(8,128)(2,1)} %all-gather.4.cloned.1.call-done, bf16[1,1024,1024]{2,1,0:T(8,128)(2,1)} %param.15), kind=kOutput, calls=%fused_computation.16 | convolution fusion | flops 2173697024 | bytes 10493952 | tf_op jit(solution)/shard_map/dot_general | solution.py:57
  90.8 1.3 copy-done.4
  92.2 4.4 %fusion.8 = f32[1024,1024]{1,0:T(8,128)} fusion(bf16[1024,1024]{0,1:T(8,128)(2,1)S(1)} %get-tuple-element.18, bf16[1,1024,1024]{2,1,0:T(8,128)(2,1)S(1)} %copy-done), kind=kOutput, calls=%fused_computation.19 | convolution fusion | flops 2147483648 | bytes 8388608 | tf_op jit(solution)/shard_map/dot_general | solution.py:70
  96.8 0.4 copy-done.3
  97.2 0.6 dynamic-slice
  98.4 5.9 %all-reduce = bf16[1024]{0:T(1024)(128)(2,1)S(1)} all-reduce(f32[1024]{0:T(1024)S(1)} %get-tuple-element.17), channel_id=3, replica_groups=mesh['expert'=8,'dp'=4] {'dp'}, use_global_device_ids=true, to_apply=%region_5.7.clone | all-reduce | flops 1024 | bytes 6144
  104.4 0.7 all_to_all.29
  105.1 5.7 %all-to-all-start.4 = ((bf16[8,1,32]{2,1,0:T(2,128)(2,1)}), bf16[8,1,32]{2,1,0:T(2,128)(2,1)S(1)}, u32[]{:S(2)}, u32[]{:S(2)}) async-start(bf16[8,1,32]{2,1,0:T(2,128)(2,1)} %all_to_all.29), calls=%async_computation.5 | async-start | bytes 8192 | tf_op jit(solution)/shard_map/all_to_all | solution.py:107
  110.8 5.9 %convert_bitcast_fusion.1 = bf16[1,1024,1024]{2,1,0:T(8,128)(2,1)} fusion(bf16[1024,1024]{1,0:T(8,128)(2,1)} %all-gather.6.cloned.1.call-done, bf16[1024,1024]{0,1:T(8,128)(2,1)} %copy-done.4), kind=kOutput, calls=%fused_computation.26 | convolution fusion | flops 2148532224 | bytes 6291456 | tf_op jit(solution)/shard_map/dot_general | solution.py:64
  116.7 24.5 %reduce-scatter.2.cloned.1.call-done = f32[256,1024]{1,0:T(8,128)} async-done(((f32[1024,1024]{1,0:T(8,128)}), f32[256,1024]{1,0:T(8,128)}) %reduce-scatter.2.cloned.1.call-update) | async-done | bytes 1048592 | tf_op jit(solution)/shard_map/reduce_scatter | solution.py:100
  141.2 2.1 %convert_element_type.34 = bf16[256,1024]{1,0:T(8,128)(2,1)} convert(f32[256,1024]{1,0:T(8,128)} %reduce-scatter.2.cloned.1.call-done) | non-fusion elementwise | flops 262144 | bytes 1572864 | tf_op jit(solution)/shard_map/convert_element_type | solution.py:103
  143.3 5.5 %all-to-all-start.3 = ((bf16[8,32,1024]{2,1,0:T(8,128)(2,1)}), bf16[8,32,1024]{2,1,0:T(8,128)(2,1)S(1)}, u32[]{:S(2)}, u32[]{:S(2)}) async-start(bf16[8,32,1024]{2,1,0:T(8,128)(2,1)} %bitcast.8), calls=%async_computation.4 | async-start | bytes 1048576 | tf_op jit(solution)/shard_map/all_to_all | solution.py:106
  148.8 7.1 %convert_bitcast_fusion = bf16[1,1024,1024]{2,1,0:T(8,128)(2,1)} fusion(bf16[1024,1024]{0,1:T(8,128)(2,1)} %all-gather.4.cloned.1.call-done, f32[1024]{0:T(1024)S(1)} %bitcast.36, f32[1024,1024]{0,1:T(8,128)} %fusion.10), kind=kOutput, calls=%fused_computation.25 | convolution fusion | flops 2161115136 | bytes 8392704 | tf_op jit(solution)/shard_map/dot_general | solution.py:67
  156.0 1.9 %gather_fusion.1 = bf16[256]{0:T(256)(128)(2,1)S(1)} fusion(bf16[256]{0:T(256)(128)(2,1)S(1)} %reshape.100, s32[1024]{0:T(1024)S(1)} %pad_clamp_fusion), kind=kCustom, calls=%fused_computation.3 | custom fusion | bytes 2048 | tf_op jit(solution)/shard_map/jit(_take)/gather | solution.py:113
  158.1 0.5 broadcast_select_fusion.3
  158.8 4.5 %all-to-all-done.3 = bf16[8,32,1024]{2,1,0:T(8,128)(2,1)S(1)} async-done(((bf16[8,32,1024]{2,1,0:T(8,128)(2,1)}), bf16[8,32,1024]{2,1,0:T(8,128)(2,1)S(1)}, u32[]{:S(2)}, u32[]{:S(2)}) %all-to-all-start.3) | async-done | bytes 524320 | tf_op jit(solution)/shard_map/all_to_all | solution.py:106
  163.3 1.2 gather_fusion
  164.5 0.2 reshape.118
  164.7 1.9 %fusion.15 = bf16[128,1024]{1,0:T(8,128)(2,1)} fusion(bf16[128,2,1024]{2,1,0:T(2,128)(2,1)S(1)} %reshape.118, pred[128,2]{1,0:T(8,128)(4,1)S(1)} %copy.31), kind=kLoop, calls=%fused_computation.29 | loop fusion | flops 393216 | bytes 786688 | tf_op jit(solution)/shard_map/reduce_sum | solution.py:112
  (39 shorter events, 1.9 us)
Async XLA Ops:
  7.2 65.9 %copy-start = (bf16[1,1024,1024]{2,1,0:T(8,128)(2,1)S(1)}, bf16[1,1024,1024]{2,1,0:T(8,128)(2,1)}, u32[]{:S(2)}) copy-start(bf16[1,1024,1024]{2,1,0:T(8,128)(2,1)} %param.14) | copy-start | bytes 6291460
  7.2 5.3 %copy-start.1 = (bf16[128,1024]{1,0:T(8,128)(2,1)S(1)}, bf16[128,1024]{1,0:T(8,128)(2,1)}, u32[]{:S(2)}) copy-start(bf16[128,1024]{1,0:T(8,128)(2,1)} %param.10) | copy-start | bytes 786436
  7.2 65.9 %all-gather.6.cloned.1.call-start = ((), (), s32[]{:S(2)}) async-start(), calls=%async_computation.7 | async-start | bytes 2621440 | tf_op jit(solution)/shard_map/all_gather | solution.py:92
  13.7 41.5 %copy-start.2 = (bf16[128,2]{0,1:T(2,128)(2,1)S(1)}, bf16[128,2]{0,1:T(2,128)(2,1)}, u32[]{:S(2)}) copy-start(bf16[128,2]{0,1:T(2,128)(2,1)} %param.13) | copy-start | bytes 1540
  36.4 46.8 %all-gather.4.cloned.1.call-start = ((), (), s32[]{:S(2)}) async-start(), calls=%async_computation.6 | async-start | bytes 2621440 | tf_op jit(solution)/shard_map/all_gather | solution.py:93
  55.2 86.0 %reduce-scatter.2.cloned.1.call-start = ((), (), s32[]{:S(2)}) async-start(), calls=%async_computation.8 | async-start | bytes 5242880 | tf_op jit(solution)/shard_map/reduce_scatter | solution.py:100
  90.8 1.3 copy-start.4
  96.5 0.7 copy-start.3
  105.1 38.2 %all-to-all-start.4 = ((bf16[8,1,32]{2,1,0:T(2,128)(2,1)}), bf16[8,1,32]{2,1,0:T(2,128)(2,1)S(1)}, u32[]{:S(2)}, u32[]{:S(2)}) async-start(bf16[8,1,32]{2,1,0:T(2,128)(2,1)} %all_to_all.29), calls=%async_computation.5 | async-start | bytes 8192 | tf_op jit(solution)/shard_map/all_to_all | solution.py:107
  143.3 20.0 %all-to-all-start.3 = ((bf16[8,32,1024]{2,1,0:T(8,128)(2,1)}), bf16[8,32,1024]{2,1,0:T(8,128)(2,1)S(1)}, u32[]{:S(2)}, u32[]{:S(2)}) async-start(bf16[8,32,1024]{2,1,0:T(8,128)(2,1)} %bitcast.8), calls=%async_computation.4 | async-start | bytes 1048576 | tf_op jit(solution)/shard_map/all_to_all | solution.py:106
Sparse Core Ops, SparseCore 0:
  36.5 21.5 all-gather.5
  60.3 22.8 all-gather.3
  96.7 44.4 reduce-scatter.1
where the time goes:
time: 174 us; the launch traced here: 173 us
  blocking collectives  60.5 us (35%)
  waiting for transfers between devices  33.2 us (19%)
  matrix products  31 us (18%)
  local copies, waits for them, and re-layouts  16.1 us (9%)
  between operations  14.6 us (8%)
  starting transfers between devices  11.3 us (6%)
  other arithmetic  6.42 us (4%)
    reduce_scatter x1, waiting for transfers between devices, per_device(): lax.psum_scatter(partial_value, 'dp', scatter_dimension=0, tiled=True)  24.5 us
    all_to_all x1, blocking collectives, per_device(): lax.all_to_all(dispatched, 'expert', split_axis=0, concat_axis=0, tiled=T...  21.7 us
    all_to_all x1, blocking collectives, per_device(): lax.all_to_all(cotangent, 'expert', split_axis=0, concat_axis=0, tiled=True)  17.7 us
    all_to_all x1, blocking collectives, per_device(): lax.all_to_all(gate_slots, 'expert', split_axis=0, concat_axis=0, tiled=T...  9.89 us
    dot_general x1, matrix products, expert_work(): lax.dot_general(slot_cot, layer_out, (((1,), (1,)), ((), ())), preferred_...  7.67 us
    dot_general x1, matrix products, expert_work(): lax.dot_general(activation, scaled, (((0,), (0,)), ((), ())), preferred_e...  7.08 us
    unnamed x1, blocking collectives  5.94 us
    dot_general x1, matrix products, expert_work(): lax.dot_general(slot_in, hidden_grad, (((0,), (0,)), ((), ())), preferred...  5.92 us
  transfers between devices with their start and end apart: 5, of which 3 were waited for; matrix products, arithmetic and copies ran while one was open for 16% of the time, Pallas kernels for 0%

commit v1 on v0

--- a/solution.py
+++ b/solution.py
@@ -1,8 +1,11 @@
+import functools
 import math
 
 import jax
 import jax.numpy as jnp
 from jax import lax
+from jax.experimental import pallas as pl
+from jax.experimental.pallas import tpu as pltpu
 from jax.sharding import PartitionSpec as P
 
 coef_root = math.sqrt(2.0 / math.pi)
@@ -114,6 +117,298 @@
     return (input_grad, gate_grad, first_grad[None], second_grad[None])
 
 
+SEND, ACROSS, BESIDE, PASS_ON, ADD_BESIDE, ADD_ACROSS, RETURN = range(7)
+
+
+def fused_kernel(
+    experts, capacity,
+    in_ref, cot_ref, ids_ref, slots_ref, gate_ref, w1_hbm, w2_hbm,
+    dx_ref, dgate_ref, dw1_hbm, dw2_hbm,
+    w1, w2, pick, packed, slots, act, hidden, scaled, inner, part,
+    got_beside, to_across, got_across, to_return, got_return, dw1, dw2,
+    send_sem, recv_sem, load_sem, store_sem,
+):
+    f32, bf16 = jnp.float32, jnp.bfloat16
+    width = in_ref.shape[1]
+    hid = w1.shape[1]
+    tile = 256
+    pad = 128
+    expert, dp = lax.axis_index("expert"), lax.axis_index("dp")
+    core, half = dp % 2, dp // 2
+    beside = dp + 1 - 2 * core
+    across = (dp + 2) % 4
+    mine = core * 2 + half
+    from_across = core * 2 + 1 - half
+    rows = 4 * capacity
+
+    def peer(d):
+        total, bit = 0, 1
+        while bit < experts:
+            total = total + ((expert // bit) % 2 + (d // bit) % 2) % 2 * bit
+            bit *= 2
+        return total
+
+    def at(start, count, step):
+        return pl.ds(pl.multiple_of(start, step), count)
+
+    def block(ref, d, q):
+        return ref.at[at(d * rows + q * capacity, capacity, capacity)]
+
+    def remote(kind, d):
+        if kind == SEND:
+            src, dst = packed.at[at(d * capacity, capacity, capacity)], block(slots, d, mine)
+            target = (peer(d), dp)
+        elif kind in (ACROSS, BESIDE):
+            src = dst = block(slots, d, mine)
+            target = (expert, across if kind == ACROSS else beside)
+        elif kind == PASS_ON:
+            src = dst = block(slots, d, from_across)
+            target = (expert, beside)
+        elif kind == ADD_BESIDE:
+            src = part.at[at(d * rows + (1 - core) * 2 * capacity, 2 * capacity, capacity)]
+            dst = got_beside.at[at(d * 2 * capacity, 2 * capacity, capacity)]
+            target = (expert, beside)
+        elif kind == ADD_ACROSS:
+            src = to_across.at[at(d * capacity, capacity, capacity)]
+            dst = got_across.at[at(d * capacity, capacity, capacity)]
+            target = (expert, across)
+        else:
+            src = to_return.at[at(d * capacity, capacity, capacity)]
+            dst = got_return.at[at(d * capacity, capacity, capacity)]
+            target = (peer(d), dp)
+        return pltpu.make_async_remote_copy(
+            src_ref=src, dst_ref=dst,
+            send_sem=send_sem.at[kind, d], recv_sem=recv_sem.at[kind, d],
+            device_id=target, device_id_type=pl.DeviceIdType.MESH,
+        )
+
+    barrier = pltpu.get_barrier_semaphore()
+    for d in range(1, experts):
+        pl.semaphore_signal(barrier, inc=1, device_id=(peer(d), dp), device_id_type=pl.DeviceIdType.MESH)
+    for other in (across, beside):
+        pl.semaphore_signal(barrier, inc=1, device_id=(expert, other), device_id_type=pl.DeviceIdType.MESH)
+    load1 = pltpu.make_async_copy(w1_hbm.at[0], w1, load_sem.at[0])
+    load2 = pltpu.make_async_copy(w2_hbm.at[0], w2, load_sem.at[1])
+    load1.start()
+    load2.start()
+
+    total = experts * capacity
+    column = lax.broadcasted_iota(jnp.int32, (in_ref.shape[0], total), 1)
+    masks = []
+    for k in range(2):
+        slot = slots_ref[:, k : k + 1]
+        place = jnp.where(slot >= 0, ids_ref[:, k : k + 1] * capacity + slot, total)
+        masks.append((place ^ (expert * capacity)) == column)
+    ones = [jnp.where(m, 1.0, 0.0).astype(f32) for m in masks]
+    pick[0] = ones[0].astype(bf16)
+    pick[1] = ones[1].astype(bf16)
+    both = (ones[0] + ones[1]).astype(bf16)
+    gates = (
+        ones[0] * gate_ref[:, 0:1].astype(f32) + ones[1] * gate_ref[:, 1:2].astype(f32)
+    ).astype(bf16)
+    along = (((0,), (0,)), ((), ()))
+    packed[:, 0:width] = lax.dot_general(both, in_ref[...], along, preferred_element_type=f32).astype(bf16)
+    packed[:, width : 2 * width] = lax.dot_general(both, cot_ref[...], along, preferred_element_type=f32).astype(bf16)
+    packed[:, 2 * width :] = lax.dot_general(
+        gates, jnp.ones((in_ref.shape[0], pad), bf16), along, preferred_element_type=f32
+    ).astype(bf16)
+    slots[at(mine * capacity, capacity, capacity)] = packed[0:capacity]
+
+    pl.semaphore_wait(barrier, experts + 1)
+    remote(ACROSS, 0).start()
+    remote(BESIDE, 0).start()
+    for d in range(experts - 1, 0, -1):
+        remote(SEND, d).start()
+
+    pairs = experts // 2
+
+    def forward(p):
+        for d in (2 * p, 2 * p + 1):
+            if d > 0:
+                remote(SEND, d).wait_recv()
+                remote(ACROSS, d).start()
+                remote(BESIDE, d).start()
+
+    def pass_on(p):
+        for d in (2 * p, 2 * p + 1):
+            remote(ACROSS, d).wait_recv()
+            remote(PASS_ON, d).start()
+
+    def compute(p):
+        for d in (2 * p, 2 * p + 1):
+            remote(BESIDE, d).wait_recv()
+            remote(PASS_ON, d).wait_recv()
+        span = slice(2 * p * rows, (2 * p + 2) * rows)
+        inner[...] = jnp.zeros_like(inner)
+
+        @pl.loop(0, hid // tile)
+        def _(n):
+            cols = at(n * tile, tile, tile)
+            pre = jnp.dot(slots[span, 0:width], w1[:, cols], preferred_element_type=f32)
+            back = lax.dot_general(
+                slots[span, width : 2 * width], w2[cols, :], (((1,), (1,)), ((), ())),
+                preferred_element_type=f32,
+            )
+            activation, derivative = gelu_pair(pre)
+            activation = activation.astype(bf16)
+            gate = slots[span, 2 * width :].astype(f32)[:, 0:1]
+            act[span, cols] = activation
+            hidden[span, cols] = (gate * back * derivative).astype(bf16)
+            product = activation.astype(f32) * back
+            inner[...] += product[:, 0:pad] + product[:, pad:]
+
+        gate = slots[span, 2 * width :].astype(f32)[:, 0:1]
+        scaled[span, :] = (gate * slots[span, width : 2 * width].astype(f32)).astype(bf16)
+
+        @pl.loop(0, width // tile)
+        def _(n):
+            cols = at(n * tile, tile, tile)
+            part[span, cols] = lax.dot_general(
+                hidden[span, :], w1[cols, :], (((1,), (1,)), ((), ())), preferred_element_type=f32
+            ).astype(bf16)
+
+        part[span, width:] = jnp.broadcast_to(
+            jnp.sum(inner[...], axis=1, keepdims=True), inner.shape
+        ).astype(bf16)
+        for d in (2 * p, 2 * p + 1):
+            remote(ADD_BESIDE, d).start()
+
+    def chip_sum(d, x):
+        return (
+            part[at(d * rows + (core * 2 + x) * capacity, capacity, capacity)].astype(f32)
+            + got_beside[at(d * 2 * capacity + x * capacity, capacity, capacity)].astype(f32)
+        )
+
+    def add_across(p):
+        for d in (2 * p, 2 * p + 1):
+            remote(ADD_BESIDE, d).wait_recv()
+            to_across[d * capacity : (d + 1) * capacity] = chip_sum(d, 1 - half).astype(bf16)
+            remote(ADD_ACROSS, d).start()
+
+    def give_back(p):
+        for d in (2 * p, 2 * p + 1):
+            span = slice(d * capacity, (d + 1) * capacity)
+            remote(ADD_ACROSS, d).wait_recv()
+            whole = (chip_sum(d, half) + got_across[span].astype(f32)).astype(bf16)
+            if d == 0:
+                got_return[span] = whole
+            else:
+                to_return[span] = whole
+                remote(RETURN, d).start()
+
+    def weight_tile(which, n):
+        cols = at(n * tile, tile, tile)
+        if which == 0:
+            dw1[cols, :] = lax.dot_general(
+                slots[:, cols], hidden[...], along, preferred_element_type=f32
+            ).astype(bf16)
+        else:
+            dw2[cols, :] = lax.dot_general(
+                act[:, cols], scaled[...], along, preferred_element_type=f32
+            ).astype(bf16)
+
+    def weight_grad(which):
+        @pl.loop(0, (width if which == 0 else hid) // tile)
+        def _(n):
+            weight_tile(which, n)
+
+        store = pltpu.make_async_copy(
+            (dw1, dw2)[which], (dw1_hbm, dw2_hbm)[which].at[0], store_sem.at[which]
+        )
+        store.start()
+        return store
+
+    forward(0)
+    load1.wait()
+    load2.wait()
+    if pairs > 1:
+        forward(1)
+    pass_on(0)
+    for p in range(pairs):
+        compute(p)
+        if p + 2 < pairs:
+            forward(p + 2)
+        if p + 1 < pairs:
+            pass_on(p + 1)
+        if p >= 1:
+            add_across(p - 1)
+        if p >= 2:
+            give_back(p - 2)
+    add_across(pairs - 1)
+    if pairs > 1:
+        give_back(pairs - 2)
+    store1 = weight_grad(0)
+    give_back(pairs - 1)
+    store2 = weight_grad(1)
+
+    for d in range(1, experts):
+        remote(RETURN, d).wait_recv()
+    both = pick[0] + pick[1]
+    dx_ref[...] = jnp.dot(both, got_return[:, 0:width], preferred_element_type=f32).astype(bf16)
+    sides = [
+        jnp.dot(pick[k], got_return[:, width:], preferred_element_type=f32)[:, 0:2] for k in range(2)
+    ]
+    lane = lax.broadcasted_iota(jnp.int32, sides[0].shape, 1)
+    dgate_ref[...] = jnp.where(lane == 0, sides[0], sides[1]).astype(bf16)
+
+    for d in range(experts):
+        for kind in range(7):
+            if d > 0 or kind not in (SEND, RETURN):
+                remote(kind, d).wait_send()
+    store1.wait()
+    store2.wait()
+
+
+def fused(inputs, out_grad, expert_ids, slot_ids, gate_values, first_layer, second_layer):
+    experts = lax.axis_size("expert")
+    tokens, width = inputs.shape
+    capacity = expert_ids.shape[1] * tokens // experts
+    hid = first_layer.shape[2]
+    total = experts * capacity
+    bf16, f32 = jnp.bfloat16, jnp.float32
+    vmem = pl.BlockSpec(memory_space=pltpu.VMEM)
+    hbm = pl.BlockSpec(memory_space=pl.ANY)
+    flops = 10 * 4 * total * width * hid
+    return pl.pallas_call(
+        functools.partial(fused_kernel, experts, capacity),
+        out_shape=(
+            jax.ShapeDtypeStruct(inputs.shape, bf16),
+            jax.ShapeDtypeStruct(gate_values.shape, bf16),
+            jax.ShapeDtypeStruct(first_layer.shape, bf16),
+            jax.ShapeDtypeStruct(second_layer.shape, bf16),
+        ),
+        in_specs=[vmem] * 5 + [hbm] * 2,
+        out_specs=(vmem, vmem, hbm, hbm),
+        scratch_shapes=[
+            pltpu.VMEM((width, hid), bf16),
+            pltpu.VMEM((hid, width), bf16),
+            pltpu.VMEM((2, tokens, total), bf16),
+            pltpu.VMEM((total, 2 * width + 128), bf16),
+            pltpu.VMEM((4 * total, 2 * width + 128), bf16),
+            pltpu.VMEM((4 * total, hid), bf16),
+            pltpu.VMEM((4 * total, hid), bf16),
+            pltpu.VMEM((4 * total, width), bf16),
+            pltpu.VMEM((8 * capacity, 128), f32),
+            pltpu.VMEM((4 * total, width + 128), bf16),
+            pltpu.VMEM((2 * total, width + 128), bf16),
+            pltpu.VMEM((total, width + 128), bf16),
+            pltpu.VMEM((total, width + 128), bf16),
+            pltpu.VMEM((total, width + 128), bf16),
+            pltpu.VMEM((total, width + 128), bf16),
+            pltpu.VMEM((width, hid), bf16),
+            pltpu.VMEM((hid, width), bf16),
+            pltpu.SemaphoreType.DMA((7, experts)),
+            pltpu.SemaphoreType.DMA((7, experts)),
+            pltpu.SemaphoreType.DMA((2,)),
+            pltpu.SemaphoreType.DMA((2,)),
+        ],
+        compiler_params=pltpu.CompilerParams(
+            collective_id=0, has_side_effects=True, vmem_limit_bytes=56 * 1024 * 1024
+        ),
+        cost_estimate=pl.CostEstimate(flops=flops, bytes_accessed=16 * width * hid, transcendentals=4 * total * hid),
+    )(inputs, out_grad, expert_ids, slot_ids, gate_values, first_layer, second_layer)
+
+
 def solution(mesh):
     placed = (
         P(("expert", "dp"), None),
@@ -124,8 +419,16 @@
         P("expert", None, "dp"),
         P("expert", "dp", None),
     )
+    experts = mesh.shape["expert"]
+
+    def chosen(inputs, out_grad, expert_ids, *rest):
+        capacity = expert_ids.shape[1] * inputs.shape[0] // experts
+        fits = capacity % 16 == 0 and experts & (experts - 1) == 0 and experts > 1
+        fits = fits and mesh.shape["dp"] == 4 and capacity & (capacity - 1) == 0
+        return (fused if fits else per_device)(inputs, out_grad, expert_ids, *rest)
+
     return jax.shard_map(
-        per_device,
+        chosen,
         mesh=mesh,
         in_specs=placed,
         out_specs=(

time: 174 us -> 84.2 us (0.48)
  Pallas kernels: 0 us -> 70.7 us
  blocking collectives: 60.5 us -> 0 us
  waiting for transfers between devices: 33.2 us -> 0 us
  matrix products: 31 us -> 0 us
  between operations: 14.6 us -> 0.64 us
  starting transfers between devices: 11.3 us -> 0 us
  other arithmetic: 6.42 us -> 0 us
  local copies, waits for them, and re-layouts: 16.1 us -> 11.8 us
    pallas_call x0 -> x1, Pallas kernels: none -> 70.7 us  [fused(): pl.pallas_call(functools.partial(fused_kernel, experts, capacity), out_sh...]
    all_to_all x3 -> x0, blocking collectives: 49.3 us -> none  [the longest x1 21.7 us: per_device(): lax.all_to_all(dispatched, 'expert', split_axis=0, concat_axis=0, tiled=T...]
    dot_general x5 -> x0, matrix products: 31 us -> none  [the longest x1 7.67 us: expert_work(): lax.dot_general(slot_cot, layer_out, (((1,), (1,)), ((), ())), preferred_...]
    reduce_scatter x1 -> x0, waiting for transfers between devices: 24.5 us -> none  [per_device(): lax.psum_scatter(partial_value, 'dp', scatter_dimension=0, tiled=True)]
    all_to_all x2 -> x0, starting transfers between devices: 11.2 us -> none  [the longest x1 5.65 us: per_device(): lax.all_to_all(slot_inner, 'expert', split_axis=0, concat_axis=0, tiled=T...]
    unnamed x14 -> x8, local copies, waits for them, and re-layouts: 2.58 us -> 10.4 us
    gather x7 -> x0, local copies, waits for them, and re-layouts: 7.18 us -> none  [the longest x1 2.54 us: build_slots(): jnp.take(inputs, owner_table, axis=0, mode='fill', fill_value=0)]
    unnamed x1 -> x0, blocking collectives: 5.94 us -> none
  transfers between devices with their start and end apart: 5 -> 0, of which waited for: 3 -> 0; matrix products, arithmetic and copies ran while one was open for 16% -> 0% of each run, Pallas kernels for 0% -> 0%
where the time goes in v1:
time: 84.2 us; the launch traced here: 83.2 us
  Pallas kernels  70.7 us (84%)
  local copies, waits for them, and re-layouts  11.8 us (14%)
    pallas_call x1, Pallas kernels, fused(): pl.pallas_call(functools.partial(fused_kernel, experts, capacity), out_sh...  70.7 us
    unnamed x8, local copies, waits for them, and re-layouts  10.4 us

profile of v1, /device:TPU:0, one launch (start us, length us, event | category | flops | bytes accessed | tf_op | source)
XLA Modules:
  0.0 83.2 jit_solution(18293105791932744248)
XLA Ops:
  0.6 1.4 %copy.13.gate_ref = bf16[128,2]{1,0:T(8,128)(2,1)} copy(bf16[128,2]{0,1:T(2,128)(2,1)} %param.11) | data formatting | bytes 1024 | tf_op args[4]
  2.0 1.4 %copy.11.ids_ref = s32[128,2]{1,0:T(8,128)} copy(s32[128,2]{0,1:T(2,128)} %param.9) | data formatting | bytes 2048 | tf_op args[2]
  3.4 1.4 %copy.12.slots_ref = s32[128,2]{1,0:T(8,128)} copy(s32[128,2]{0,1:T(2,128)} %param.10) | data formatting | bytes 2048 | tf_op args[3]
  4.8 70.7 %shard_map.102 = (bf16[128,1024]{1,0:T(8,128)(2,1)}, bf16[128,2]{1,0:T(8,128)(2,1)}, bf16[1,1024,1024]{2,1,0:T(8,128)(2,1)}, bf16[1,1024,1024]{2,1,0:T(8,128)(2,1)}) custom-call(bf16[128,1024]{1,0:T(8,128)(2,1)} %in_ref.1, bf16[128,1024]{1,0:T(8,128)(2,1)} %cot_ref.1, s32[128,2]{1,0:T(8,128)} %copy.11.ids_ref, s32[128,2]{1,0:T(8,128)} %copy.12.slots_ref, ...), custom_call_target="tpu_custom_call" | custom-call | flops 10737418240 | bytes 16777216 | tf_op jit(solution)/shard_map/pallas_call | solution.py:372
  75.6 1.4 %copy.14 = bf16[128,2]{0,1:T(2,128)(2,1)} copy(bf16[128,2]{1,0:T(8,128)(2,1)} %get-tuple-element.5) | data formatting | bytes 1024 | tf_op jit(solution)/shard_map/pallas_call | solution.py:372
  76.9 1.7 %copy.18 = bf16[128,1024]{1,0:T(8,128)(2,1)} copy(bf16[128,1024]{1,0:T(8,128)(2,1)} %get-tuple-element.12) | data formatting | bytes 524288
  78.6 0.0 copy-start
  78.6 3.2 %copy.19 = bf16[1,1024,1024]{2,1,0:T(8,128)(2,1)} copy(bf16[1,1024,1024]{2,1,0:T(8,128)(2,1)} %get-tuple-element.14) | data formatting | bytes 4194304
  81.8 0.0 copy-done
  81.8 1.3 %copy.20 = bf16[1,1024,1024]{2,1,0:T(8,128)(2,1)} copy(bf16[1,1024,1024]{2,1,0:T(8,128)(2,1)S(1)} %copy-done) | data formatting | bytes 4194304
Async XLA Ops:
  78.6 3.2 %copy-start = (bf16[1,1024,1024]{2,1,0:T(8,128)(2,1)S(1)}, bf16[1,1024,1024]{2,1,0:T(8,128)(2,1)}, u32[]{:S(2)}) copy-start(bf16[1,1024,1024]{2,1,0:T(8,128)(2,1)} %get-tuple-element.15) | copy-start | bytes 6291460

commit v2 on v1

--- a/solution.py
+++ b/solution.py
@@ -118,6 +118,17 @@
 
 
 SEND, ACROSS, BESIDE, PASS_ON, ADD_BESIDE, ADD_ACROSS, RETURN = range(7)
+
+
+def exchange_order(experts):
+    half = experts // 2
+    first = list(range(min(2, half)))
+    order = list(first)
+    for i in range(half):
+        order.append(half + i)
+        if len(first) + i < half:
+            order.append(len(first) + i)
+    return order
 
 
 def fused_kernel(
@@ -141,7 +152,10 @@
     from_across = core * 2 + 1 - half
     rows = 4 * capacity
 
+    offsets = exchange_order(experts)
+
     def peer(d):
+        d = offsets[d]
         total, bit = 0, 1
         while bit < experts:
             total = total + ((expert // bit) % 2 + (d // bit) % 2) % 2 * bit
@@ -156,7 +170,8 @@
 
     def remote(kind, d):
         if kind == SEND:
-            src, dst = packed.at[at(d * capacity, capacity, capacity)], block(slots, d, mine)
+            src = packed.at[at(offsets[d] * capacity, capacity, capacity)]
+            dst = block(slots, d, mine)
             target = (peer(d), dp)
         elif kind in (ACROSS, BESIDE):
             src = dst = block(slots, d, mine)
@@ -174,7 +189,7 @@
             target = (expert, across)
         else:
             src = to_return.at[at(d * capacity, capacity, capacity)]
-            dst = got_return.at[at(d * capacity, capacity, capacity)]
+            dst = got_return.at[at(offsets[d] * capacity, capacity, capacity)]
             target = (peer(d), dp)
         return pltpu.make_async_remote_copy(
             src_ref=src, dst_ref=dst,
@@ -193,31 +208,29 @@
     load2.start()
 
     total = experts * capacity
-    column = lax.broadcasted_iota(jnp.int32, (in_ref.shape[0], total), 1)
-    masks = []
+    row = lax.broadcasted_iota(jnp.int32, (total, in_ref.shape[0]), 0)
+    gate = gate_ref[...].astype(f32)
+    ones = []
     for k in range(2):
-        slot = slots_ref[:, k : k + 1]
-        place = jnp.where(slot >= 0, ids_ref[:, k : k + 1] * capacity + slot, total)
-        masks.append((place ^ (expert * capacity)) == column)
-    ones = [jnp.where(m, 1.0, 0.0).astype(f32) for m in masks]
+        slot = slots_ref[k : k + 1, :]
+        place = jnp.where(slot >= 0, ids_ref[k : k + 1, :] * capacity + slot, total)
+        ones.append(jnp.where((place ^ (expert * capacity)) == row, 1.0, 0.0).astype(f32))
     pick[0] = ones[0].astype(bf16)
     pick[1] = ones[1].astype(bf16)
     both = (ones[0] + ones[1]).astype(bf16)
-    gates = (
-        ones[0] * gate_ref[:, 0:1].astype(f32) + ones[1] * gate_ref[:, 1:2].astype(f32)
-    ).astype(bf16)
+    gates = (ones[0] * gate[0:1, :] + ones[1] * gate[1:2, :]).astype(bf16)
     along = (((0,), (0,)), ((), ()))
-    packed[:, 0:width] = lax.dot_general(both, in_ref[...], along, preferred_element_type=f32).astype(bf16)
-    packed[:, width : 2 * width] = lax.dot_general(both, cot_ref[...], along, preferred_element_type=f32).astype(bf16)
-    packed[:, 2 * width :] = lax.dot_general(
-        gates, jnp.ones((in_ref.shape[0], pad), bf16), along, preferred_element_type=f32
+    packed[:, 0:width] = jnp.dot(both, in_ref[...], preferred_element_type=f32).astype(bf16)
+    packed[:, width : 2 * width] = jnp.dot(both, cot_ref[...], preferred_element_type=f32).astype(bf16)
+    packed[:, 2 * width :] = jnp.dot(
+        gates, jnp.ones((in_ref.shape[0], pad), bf16), preferred_element_type=f32
     ).astype(bf16)
     slots[at(mine * capacity, capacity, capacity)] = packed[0:capacity]
 
     pl.semaphore_wait(barrier, experts + 1)
     remote(ACROSS, 0).start()
     remote(BESIDE, 0).start()
-    for d in range(experts - 1, 0, -1):
+    for d in range(1, experts):
         remote(SEND, d).start()
 
     pairs = experts // 2
@@ -319,11 +332,11 @@
         return store
 
     forward(0)
-    load1.wait()
-    load2.wait()
     if pairs > 1:
         forward(1)
     pass_on(0)
+    load1.wait()
+    load2.wait()
     for p in range(pairs):
         compute(p)
         if p + 2 < pairs:
@@ -344,12 +357,15 @@
     for d in range(1, experts):
         remote(RETURN, d).wait_recv()
     both = pick[0] + pick[1]
-    dx_ref[...] = jnp.dot(both, got_return[:, 0:width], preferred_element_type=f32).astype(bf16)
+    dx_ref[...] = lax.dot_general(
+        both, got_return[:, 0:width], along, preferred_element_type=f32
+    ).astype(bf16)
     sides = [
-        jnp.dot(pick[k], got_return[:, width:], preferred_element_type=f32)[:, 0:2] for k in range(2)
+        lax.dot_general(got_return[:, width:], pick[k], along, preferred_element_type=f32)[0:2]
+        for k in range(2)
     ]
-    lane = lax.broadcasted_iota(jnp.int32, sides[0].shape, 1)
-    dgate_ref[...] = jnp.where(lane == 0, sides[0], sides[1]).astype(bf16)
+    side = lax.broadcasted_iota(jnp.int32, sides[0].shape, 0)
+    dgate_ref[...] = jnp.where(side == 0, sides[0], sides[1]).astype(bf16)
 
     for d in range(experts):
         for kind in range(7):
@@ -369,11 +385,11 @@
     vmem = pl.BlockSpec(memory_space=pltpu.VMEM)
     hbm = pl.BlockSpec(memory_space=pl.ANY)
     flops = 10 * 4 * total * width * hid
-    return pl.pallas_call(
+    dx, dgate, dw1, dw2 = pl.pallas_call(
         functools.partial(fused_kernel, experts, capacity),
         out_shape=(
             jax.ShapeDtypeStruct(inputs.shape, bf16),
-            jax.ShapeDtypeStruct(gate_values.shape, bf16),
+            jax.ShapeDtypeStruct(gate_values.shape[::-1], bf16),
             jax.ShapeDtypeStruct(first_layer.shape, bf16),
             jax.ShapeDtypeStruct(second_layer.shape, bf16),
         ),
@@ -382,7 +398,7 @@
         scratch_shapes=[
             pltpu.VMEM((width, hid), bf16),
             pltpu.VMEM((hid, width), bf16),
-            pltpu.VMEM((2, tokens, total), bf16),
+            pltpu.VMEM((2, total, tokens), bf16),
             pltpu.VMEM((total, 2 * width + 128), bf16),
             pltpu.VMEM((4 * total, 2 * width + 128), bf16),
             pltpu.VMEM((4 * total, hid), bf16),
@@ -406,7 +422,8 @@
             collective_id=0, has_side_effects=True, vmem_limit_bytes=56 * 1024 * 1024
         ),
         cost_estimate=pl.CostEstimate(flops=flops, bytes_accessed=16 * width * hid, transcendentals=4 * total * hid),
-    )(inputs, out_grad, expert_ids, slot_ids, gate_values, first_layer, second_layer)
+    )(inputs, out_grad, expert_ids.T, slot_ids.T, gate_values.T, first_layer, second_layer)
+    return dx, dgate.T, dw1, dw2
 
 
 def solution(mesh):

time: 84.2 us -> 69.2 us (0.82)
  Pallas kernels: 70.7 us -> 61 us
  local copies, waits for them, and re-layouts: 11.8 us -> 7.37 us
    pallas_call x1, Pallas kernels: 70.7 us -> 61 us  [fused(): pl.pallas_call(functools.partial(fused_kernel, experts, capacity), out_sh...]
    unnamed x8 -> x6, local copies, waits for them, and re-layouts: 10.4 us -> 7.37 us
    pallas_call x1 -> x0, local copies, waits for them, and re-layouts: 1.35 us -> none  [fused(): pl.pallas_call(functools.partial(fused_kernel, experts, capacity), out_sh...]
where the time goes in v2:
time: 69.2 us; the launch traced here: 69 us
  Pallas kernels  61 us (88%)
  local copies, waits for them, and re-layouts  7.37 us (11%)
    pallas_call x1, Pallas kernels, fused(): pl.pallas_call(functools.partial(fused_kernel, experts, capacity), out_sh...  61 us
    unnamed x6, local copies, waits for them, and re-layouts  7.37 us

profile of v2, /device:TPU:0, one launch (start us, length us, event | category | flops | bytes accessed | tf_op | source)
XLA Modules:
  0.0 69.0 jit_solution(2105643758870655727)
XLA Ops:
  0.6 61.0 %shard_map.102 = (bf16[128,1024]{1,0:T(8,128)(2,1)}, bf16[2,128]{1,0:T(2,128)(2,1)}, bf16[1,1024,1024]{2,1,0:T(8,128)(2,1)}, bf16[1,1024,1024]{2,1,0:T(8,128)(2,1)}) custom-call(bf16[128,1024]{1,0:T(8,128)(2,1)} %in_ref.1, bf16[128,1024]{1,0:T(8,128)(2,1)} %cot_ref.1, s32[2,128]{1,0:T(2,128)} %bitcast.4, s32[2,128]{1,0:T(2,128)} %bitcast.5, ...), custom_call_target="tpu_custom_call" | custom-call | flops 10737418240 | bytes 16777216 | tf_op jit(solution)/shard_map/pallas_call | solution.py:388
  61.6 1.7 %copy.15 = bf16[128,1024]{1,0:T(8,128)(2,1)} copy(bf16[128,1024]{1,0:T(8,128)(2,1)} %get-tuple-element.16) | data formatting | bytes 524288
  63.3 1.1 %copy.16 = bf16[128,2]{0,1:T(2,128)(2,1)} copy(bf16[128,2]{0,1:T(2,128)(2,1)} %bitcast.7) | data formatting | bytes 1024
  64.4 0.0 copy-start
  64.4 3.2 %copy.17 = bf16[1,1024,1024]{2,1,0:T(8,128)(2,1)} copy(bf16[1,1024,1024]{2,1,0:T(8,128)(2,1)} %get-tuple-element.18) | data formatting | bytes 4194304
  67.7 0.0 copy-done
  67.7 1.3 %copy.18 = bf16[1,1024,1024]{2,1,0:T(8,128)(2,1)} copy(bf16[1,1024,1024]{2,1,0:T(8,128)(2,1)S(1)} %copy-done) | data formatting | bytes 4194304
Async XLA Ops:
  64.4 3.2 %copy-start = (bf16[1,1024,1024]{2,1,0:T(8,128)(2,1)S(1)}, bf16[1,1024,1024]{2,1,0:T(8,128)(2,1)}, u32[]{:S(2)}) copy-start(bf16[1,1024,1024]{2,1,0:T(8,128)(2,1)} %get-tuple-element.19) | copy-start | bytes 6291460

commit v3 on v2

--- a/solution.py
+++ b/solution.py
@@ -341,15 +341,11 @@
         compute(p)
         if p + 2 < pairs:
             forward(p + 2)
+        add_across(p)
         if p + 1 < pairs:
             pass_on(p + 1)
         if p >= 1:
-            add_across(p - 1)
-        if p >= 2:
-            give_back(p - 2)
-    add_across(pairs - 1)
-    if pairs > 1:
-        give_back(pairs - 2)
+            give_back(p - 1)
     store1 = weight_grad(0)
     give_back(pairs - 1)
     store2 = weight_grad(1)
@@ -373,6 +369,43 @@
                 remote(kind, d).wait_send()
     store1.wait()
     store2.wait()
+
+
+def hand_over_kernel(pieces, *refs):
+    count = len(pieces)
+    sources, results, held = refs[:count], refs[count : 2 * count], refs[2 * count : 3 * count]
+    load_sem, store_sem = refs[3 * count :]
+    moves = []
+    for i, split in enumerate(pieces):
+        height = sources[i].shape[0] // split
+        for j in range(split):
+            part = pl.ds(j * height, height)
+            n = len(moves)
+            moves.append((
+                pltpu.make_async_copy(sources[i].at[part], held[i].at[part], load_sem.at[n]),
+                pltpu.make_async_copy(held[i].at[part], results[i].at[part], store_sem.at[n]),
+            ))
+    for load, _ in moves:
+        load.start()
+    for load, store in moves:
+        load.wait()
+        store.start()
+    for _, store in moves:
+        store.wait()
+
+
+def hand_over(arrays, pieces):
+    hbm = pl.BlockSpec(memory_space=pl.ANY)
+    shapes = tuple(jax.ShapeDtypeStruct(a.shape, a.dtype) for a in arrays)
+    return pl.pallas_call(
+        functools.partial(hand_over_kernel, pieces),
+        out_shape=shapes,
+        in_specs=[hbm] * len(arrays),
+        out_specs=(hbm,) * len(arrays),
+        scratch_shapes=[pltpu.VMEM(a.shape, a.dtype) for a in arrays]
+        + [pltpu.SemaphoreType.DMA((sum(pieces),))] * 2,
+        compiler_params=pltpu.CompilerParams(vmem_limit_bytes=56 * 1024 * 1024),
+    )(*arrays)
 
 
 def fused(inputs, out_grad, expert_ids, slot_ids, gate_values, first_layer, second_layer):
@@ -423,7 +456,8 @@
         ),
         cost_estimate=pl.CostEstimate(flops=flops, bytes_accessed=16 * width * hid, transcendentals=4 * total * hid),
     )(inputs, out_grad, expert_ids.T, slot_ids.T, gate_values.T, first_layer, second_layer)
-    return dx, dgate.T, dw1, dw2
+    first_grad, second_grad, dx, dgate = hand_over((dw1[0], dw2[0], dx, dgate), (4, 4, 1, 1))
+    return dx, dgate.T, first_grad[None], second_grad[None]
 
 
 def solution(mesh):

time: 69.2 us -> 64.8 us (0.936)
  local copies, waits for them, and re-layouts: 7.37 us -> 0 us
  Pallas kernels: 61 us -> 64 us
    unnamed x6 -> x0, local copies, waits for them, and re-layouts: 7.37 us -> none
    pallas_call x0 -> x1, Pallas kernels: none -> 3.8 us  [hand_over(): pl.pallas_call(functools.partial(hand_over_kernel, pieces), out_shape=sha...]
    pallas_call x1, Pallas kernels: 61 us -> 60.2 us  [fused(): pl.pallas_call(functools.partial(fused_kernel, experts, capacity), out_sh...]
where the time goes in v3:
time: 64.8 us; the launch traced here: 64.7 us
  Pallas kernels  64 us (99%)
    pallas_call x1, Pallas kernels, fused(): pl.pallas_call(functools.partial(fused_kernel, experts, capacity), out_sh...  60.2 us
    pallas_call x1, Pallas kernels, hand_over(): pl.pallas_call(functools.partial(hand_over_kernel, pieces), out_shape=sha...  3.8 us

profile of v3, /device:TPU:0, one launch (start us, length us, event | category | flops | bytes accessed | tf_op | source)
XLA Modules:
  0.0 64.7 jit_solution(7936856387765131668)
XLA Ops:
  0.6 60.2 %shard_map.102 = (bf16[128,1024]{1,0:T(8,128)(2,1)}, bf16[2,128]{1,0:T(2,128)(2,1)}, bf16[1,1024,1024]{2,1,0:T(8,128)(2,1)}, bf16[1,1024,1024]{2,1,0:T(8,128)(2,1)}) custom-call(bf16[128,1024]{1,0:T(8,128)(2,1)} %in_ref.1, bf16[128,1024]{1,0:T(8,128)(2,1)} %cot_ref.1, s32[2,128]{1,0:T(2,128)} %bitcast.12, s32[2,128]{1,0:T(2,128)} %bitcast.13, ...), custom_call_target="tpu_custom_call" | custom-call | flops 10737418240 | bytes 16777216 | tf_op jit(solution)/shard_map/pallas_call | solution.py:421
  60.9 3.8 %shard_map.103 = (bf16[1024,1024]{1,0:T(8,128)(2,1)}, bf16[1024,1024]{1,0:T(8,128)(2,1)}, bf16[128,1024]{1,0:T(8,128)(2,1)}, bf16[2,128]{1,0:T(2,128)(2,1)}) custom-call(bf16[1024,1024]{1,0:T(8,128)(2,1)} %bitcast.8, bf16[1024,1024]{1,0:T(8,128)(2,1)} %bitcast.9, bf16[128,1024]{1,0:T(8,128)(2,1)} %get-tuple-element.14.refs_2_, ...), custom_call_target="tpu_custom_call" | custom-call | tf_op jit(solution)/shard_map/pallas_call | solution.py:400

commit v4 on v3

--- a/solution.py
+++ b/solution.py
@@ -142,7 +142,7 @@
     f32, bf16 = jnp.float32, jnp.bfloat16
     width = in_ref.shape[1]
     hid = w1.shape[1]
-    tile = 256
+    tile = 512
     pad = 128
     expert, dp = lax.axis_index("expert"), lax.axis_index("dp")
     core, half = dp % 2, dp // 2
@@ -228,10 +228,10 @@
     slots[at(mine * capacity, capacity, capacity)] = packed[0:capacity]
 
     pl.semaphore_wait(barrier, experts + 1)
+    for d in range(1, experts):
+        remote(SEND, d).start()
     remote(ACROSS, 0).start()
     remote(BESIDE, 0).start()
-    for d in range(1, experts):
-        remote(SEND, d).start()
 
     pairs = experts // 2
 
@@ -268,7 +268,7 @@
             act[span, cols] = activation
             hidden[span, cols] = (gate * back * derivative).astype(bf16)
             product = activation.astype(f32) * back
-            inner[...] += product[:, 0:pad] + product[:, pad:]
+            inner[...] += sum(product[:, c : c + pad] for c in range(0, tile, pad))
 
         gate = slots[span, 2 * width :].astype(f32)[:, 0:1]
         scaled[span, :] = (gate * slots[span, width : 2 * width].astype(f32)).astype(bf16)

time: 64.8 us -> 62.7 us (0.968)
  Pallas kernels: 64 us -> 61.8 us
    pallas_call x1, Pallas kernels: 60.2 us -> 58 us  [fused(): pl.pallas_call(functools.partial(fused_kernel, experts, capacity), out_sh...]
where the time goes in v4:
time: 62.7 us; the launch traced here: 62.4 us
  Pallas kernels  61.8 us (99%)
  between operations  0.64 us (1%)
    pallas_call x1, Pallas kernels, fused(): pl.pallas_call(functools.partial(fused_kernel, experts, capacity), out_sh...  58 us
    pallas_call x1, Pallas kernels, hand_over(): pl.pallas_call(functools.partial(hand_over_kernel, pieces), out_shape=sha...  3.8 us

profile of v4, /device:TPU:0, one launch (start us, length us, event | category | flops | bytes accessed | tf_op | source)
XLA Modules:
  0.0 62.4 jit_solution(16260337130454771475)
XLA Ops:
  0.6 58.0 %shard_map.102 = (bf16[128,1024]{1,0:T(8,128)(2,1)}, bf16[2,128]{1,0:T(2,128)(2,1)}, bf16[1,1024,1024]{2,1,0:T(8,128)(2,1)}, bf16[1,1024,1024]{2,1,0:T(8,128)(2,1)}) custom-call(bf16[128,1024]{1,0:T(8,128)(2,1)} %in_ref.1, bf16[128,1024]{1,0:T(8,128)(2,1)} %cot_ref.1, s32[2,128]{1,0:T(2,128)} %bitcast.12, s32[2,128]{1,0:T(2,128)} %bitcast.13, ...), custom_call_target="tpu_custom_call" | custom-call | flops 10737418240 | bytes 16777216 | tf_op jit(solution)/shard_map/pallas_call | solution.py:421
  58.6 3.8 %shard_map.103 = (bf16[1024,1024]{1,0:T(8,128)(2,1)}, bf16[1024,1024]{1,0:T(8,128)(2,1)}, bf16[128,1024]{1,0:T(8,128)(2,1)}, bf16[2,128]{1,0:T(2,128)(2,1)}) custom-call(bf16[1024,1024]{1,0:T(8,128)(2,1)} %bitcast.8, bf16[1024,1024]{1,0:T(8,128)(2,1)} %bitcast.9, bf16[128,1024]{1,0:T(8,128)(2,1)} %get-tuple-element.14.refs_2_, ...), custom_call_target="tpu_custom_call" | custom-call | tf_op jit(solution)/shard_map/pallas_call | solution.py:400
